TPU v7x, 256 devices: a whole 4x4x8 slice. The times are simulated.
256 devices in a mesh: dp: 4 (over y_lo, core), ctx: 64 (over y_hi, x, z).
Axes of the slice: x: 4, y: 4 (y_hi: 2, y_lo: 2; y = y_hi * 2 + y_lo), z: 8, core: 2. Of those that a mesh axis runs over, the one named last changes fastest.
Arguments:
- query: bfloat16 [4, 16384, 4096], P('dp', 'ctx'), may hold values from -6 to 6
- key_proj: bfloat16 [4, 16384, 512], P('dp', 'ctx'), may hold values from -6 to 6
- value: bfloat16 [4, 16384, 512], P('dp', 'ctx'), may hold values from -6 to 6
- sinks: float32 [64], replicated, may hold values from 0 to 6
- doc_ids: int32 [4, 16384], P('dp'), may hold values from 0 to 63, never falling along the last dimension, each value on 1 to 512 neighbouring positions
- grad_out: bfloat16 [4, 16384, 4096], P('dp', 'ctx'), may hold values from -6 to 6
Outputs:
- attended: bfloat16 [4, 16384, 4096], P('dp', 'ctx')
- grad_query: bfloat16 [4, 16384, 4096], P('dp', 'ctx')
- grad_key: bfloat16 [4, 16384, 512], P('dp', 'ctx')
- grad_value: bfloat16 [4, 16384, 512], P('dp', 'ctx')
- grad_sinks: float32 [64], replicated
Inputs may be any that keep to these rules, and one draw needn't show every extreme that they name: `doc_ids`: each trace's documents are contiguous runs of tokens, numbered upward, each at most 512 tokens long, one exactly so.
All inputs are finite; a program needn't handle non-finite values.
Results may differ from a plain program's by a relative error of at most 0.012.
The roundings to bfloat16 on the way count: a program that leaves them out, or rounds other values in their place, can miss the bound.
Values may be sent and summed in bfloat16 or wider, within the bound.
No kernel may reach another device: no remote copies, remote signals or barrier semaphores. Data moves between devices by JAX's collectives and lax.ppermute only.
A program may use at most 128 MiB of HBM per device.

v0:
```python
import functools

import jax
import jax.numpy as jnp
from jax import lax
from jax.experimental import pallas as pl
from jax.experimental.pallas import tpu as pltpu
from jax.sharding import PartitionSpec as P

H = 64
KV = 8
HD = 64
SPAN = 2
ROWS = 256
TILE = 128
WIN = SPAN * ROWS + TILE
CHUNKS = 2
PAIRS = KV // 2
FAR = 16384.0

score_scale = 0.125


def passed_along(block, axis, distance):
    devices = range(lax.axis_size(axis))
    route = [(i - distance, i) for i in devices if i - distance in devices]
    return lax.ppermute(block, axis, route)


def dot(a, b, dim_a, dim_b):
    return lax.dot_general(
        a, b, (((dim_a,), (dim_b,)), ((), ())), preferred_element_type=jnp.float32
    )


def side_by_side(x):
    return jnp.concatenate([x[:HD], x[HD:]], axis=1)


def stacked(x):
    return jnp.concatenate([x[:, :TILE], x[:, TILE:]], axis=0)


def kernel(first, *refs):
    if not first:
        refs = refs[:8] + refs[10:]
    (q_ref, g_ref, kv2_ref, kv1_ref, kv0_ref, f_ref, t_ref, s_ref) = refs[:8]
    (o_ref, dq_ref, d2_ref, d1_ref, d0_ref, sg_ref) = refs[8:14]
    (kk, vv, kt, vt, pr, pt, dst, qm, gm, acck, accv) = refs[14:]
    lane = lax.broadcasted_iota(jnp.int32, (TILE, 2 * HD), 1)
    even = lane < HD
    key_at = lax.broadcasted_iota(jnp.int32, (TILE, 2 * TILE), 0)
    query_at = lax.broadcasted_iota(jnp.int32, (TILE, 2 * TILE), 1) % TILE
    causal = key_at <= query_at
    for n, ref in enumerate((kv2_ref, kv1_ref, kv0_ref)):
        kt[:, n * ROWS : (n + 1) * ROWS] = ref[:, : 2 * HD].T
        vt[:, n * ROWS : (n + 1) * ROWS] = ref[:, 2 * HD :].T
    for h in range(2):
        kk[h, :, 2 * HD :] = t_ref[...]
        for n, ref in enumerate((kv2_ref, kv1_ref, kv0_ref)):
            k_head = ref[:, h * HD : (h + 1) * HD]
            v_head = ref[:, (2 + h) * HD : (3 + h) * HD]
            rows = slice(n * ROWS, (n + 1) * ROWS)
            kk[h, rows, :HD] = k_head
            kk[h, rows, HD : 2 * HD] = k_head
            vv[h, rows, :HD] = v_head
            vv[h, rows, HD:] = v_head

    def places(n):
        h, r = divmod(n, 2)
        rows = slice(r * TILE, (r + 1) * TILE)
        win = slice(r * TILE, r * TILE + WIN)
        return h, r, rows, win, slice(h * HD, (h + 1) * HD)

    def columns(h, p):
        lanes = slice(h * 512 + p * 128, h * 512 + (p + 1) * 128)
        return lanes, slice(p * 2 * TILE, (p + 1) * 2 * TILE), slice(h * 4 + p, h * 4 + p + 1)

    def apart(x):
        zero = jnp.zeros_like(x)
        return jnp.concatenate([jnp.where(even, x, zero), jnp.where(even, zero, x)], 0)

    kept = {}

    def softmax(n):
        h, r, rows, win, own = places(n)
        f = f_ref[rows, :]
        f = jnp.concatenate([f, f], 0)
        kept[n % 3] = []
        for p in range(4):
            lanes, cols, line = columns(h, p)
            rq = apart(q_ref[rows, lanes] * jnp.bfloat16(score_scale))
            qm[n % 3, cols, :] = rq
            s = dot(kk[h, win, :], jnp.concatenate([rq, f], 1), 1, 1)
            s = jnp.concatenate([s[: WIN - TILE], jnp.where(causal, s[WIN - TILE :], -FAR)], 0)
            sink = s_ref[line, :]
            top = jnp.maximum(jnp.max(s, axis=0, keepdims=True), sink)
            expo = jnp.exp(s - top)
            sink_part = jnp.exp(sink - top)
            share = 1.0 / (jnp.sum(expo, axis=0, keepdims=True) + sink_part)
            probs = expo * share
            pr[n % 3, :, cols] = probs
            pt[n % 3, :, cols] = probs.astype(jnp.bfloat16)
            kept[n % 3].append(sink_part * share)

    def attended(n):
        h, r, rows, win, own = places(n)
        out = dot(vt[own, win], pt[n % 3], 1, 0).astype(jnp.bfloat16)
        kept[n % 3, "out"] = out.astype(jnp.float32)

    def grad_scores(n):
        h, r, rows, win, own = places(n)
        for p in range(4):
            lanes, cols, line = columns(h, p)
            gp = g_ref[rows, lanes]
            rg = apart(gp)
            gm[n % 3, cols, :] = rg
            out = kept[n % 3, "out"][:, cols]
            g_t = side_by_side(gp.astype(jnp.float32).T)
            rowdot = jnp.sum(g_t * out, axis=0, keepdims=True)
            o_ref[rows, lanes] = stacked(out).T.astype(jnp.bfloat16)
            dp = dot(vv[h, win, :], rg, 1, 1)
            dst[n % 3, :, cols] = (pr[n % 3, :, cols] * (dp - rowdot)).astype(jnp.bfloat16)
            sink_grad = -(kept[n % 3][p] * rowdot)
            if r == 0:
                sg_ref[line, :] = sink_grad
            else:
                sg_ref[line, :] += sink_grad

    def grad_query(n):
        h, r, rows, win, own = places(n)
        dq = dot(kt[own, win], dst[n % 3], 1, 0) * score_scale
        for p in range(4):
            lanes, cols, line = columns(h, p)
            dq_ref[rows, lanes] = stacked(dq[:, cols]).T.astype(jnp.bfloat16)

    def gathered(n, acc, big, small):
        h, r, rows, win, own = places(n)
        part = dot(big[n % 3], small[n % 3], 1, 0)
        if r == 0:
            acc[h, :WIN, :] = part
        else:
            acc[h, TILE:WIN, :] += part[: WIN - TILE]
            acc[h, WIN:, :] = part[WIN - TILE :]

    softmax(0)
    for n in range(4):
        if n < 3:
            softmax(n + 1)
        attended(n)
        if n > 0:
            grad_query(n - 1)
            gathered(n - 1, acck, dst, qm)
        grad_scores(n)
        gathered(n, accv, pt, gm)
    grad_query(3)
    gathered(3, acck, dst, qm)

    lane = lax.broadcasted_iota(jnp.int32, (ROWS, 2 * HD), 1)
    for side, acc in ((0, acck), (1, accv)):
        cols = slice(side * 2 * HD, (side + 1) * 2 * HD)
        for n, ref in enumerate((d2_ref, d1_ref, d0_ref)):
            a = acc[0, n * ROWS : (n + 1) * ROWS, :]
            b = acc[1, n * ROWS : (n + 1) * ROWS, :]
            a = a + pltpu.roll(a, HD, 1)
            b = b + pltpu.roll(b, HD, 1)
            ref[:, cols] = jnp.where(lane < HD, a, b).astype(ref.dtype)


def attend(chunk, queries, grads, kv, f, t, sink_rows, so_far):
    bf, f32 = jnp.bfloat16, jnp.float32
    steps = PAIRS // CHUNKS
    base = chunk * steps
    wide = pl.BlockSpec((ROWS, 1024), lambda i: (0, base + i))
    pair = pl.BlockSpec((ROWS, 256), lambda i: (0, i))
    small = pl.BlockSpec((8, 256), lambda i: (base + i, 0))
    whole = pl.BlockSpec(memory_space=pl.ANY)
    in_specs = [wide, wide, pair, pair, pair]
    in_specs += [pl.BlockSpec((ROWS, 128), lambda i: (0, 0))]
    in_specs += [pl.BlockSpec((3 * ROWS, 128), lambda i: (0, 0)), small]
    queries = pltpu.with_memory_space_constraint(queries, pltpu.HBM)
    grads = pltpu.with_memory_space_constraint(grads, pltpu.HBM)
    args = (queries, grads, *kv, f, t, sink_rows)
    aliases = {}
    if so_far is not None:
        in_specs += [whole, whole]
        args += so_far
        aliases = {8: 0, 9: 1}
    return pl.pallas_call(
        functools.partial(kernel, so_far is None),
        grid=(steps,),
        in_specs=in_specs,
        out_specs=[wide, wide, pair, pair, pair, pl.BlockSpec((8, 256), lambda i: (i, 0))],
        out_shape=[
            pltpu.HBM((ROWS, H * HD), bf),
            pltpu.HBM((ROWS, H * HD), bf),
            jax.ShapeDtypeStruct((ROWS, 256 * steps), bf),
            jax.ShapeDtypeStruct((ROWS, 256 * steps), bf),
            jax.ShapeDtypeStruct((ROWS, 256 * steps), f32),
            jax.ShapeDtypeStruct((8 * steps, 256), f32),
        ],
        scratch_shapes=[
            pltpu.VMEM((2, 3 * ROWS, 256), bf),
            pltpu.VMEM((2, 3 * ROWS, 128), bf),
            pltpu.VMEM((128, 3 * ROWS), bf),
            pltpu.VMEM((128, 3 * ROWS), bf),
            pltpu.VMEM((3, WIN, 1024), f32),
            pltpu.VMEM((3, WIN, 1024), bf),
            pltpu.VMEM((3, WIN, 1024), bf),
            pltpu.VMEM((3, 1024, 128), bf),
            pltpu.VMEM((3, 1024, 128), bf),
            pltpu.VMEM((2, 3 * ROWS, 128), f32),
            pltpu.VMEM((2, 3 * ROWS, 128), f32),
        ],
        input_output_aliases=aliases,
        cost_estimate=pl.CostEstimate(
            flops=steps * 16 * 6 * 2 * 256 * WIN * ROWS,
            transcendentals=steps * 16 * WIN * ROWS,
            bytes_accessed=steps * 4 * 1024 * ROWS,
        ),
        compiler_params=pltpu.CompilerParams(vmem_limit_bytes=36 * 1024 * 1024),
    )(*args)


def on_device(query, key_proj, value, sinks, doc_ids, grad_out):
    queries, keys, values, grads = query[0], key_proj[0], value[0], grad_out[0]
    steps = PAIRS // CHUNKS
    own = []
    for c in range(CHUNKS):
        parts = []
        for i in range(c * steps, (c + 1) * steps):
            parts += [keys[:, i * 128 : (i + 1) * 128], values[:, i * 128 : (i + 1) * 128]]
        own.append(jnp.concatenate(parts, axis=1))
    near = [passed_along(x, "ctx", 1) for x in own]
    far = []
    for c, x in enumerate(near):
        if c > 0:
            x, far[c - 1] = lax.optimization_barrier((x, far[c - 1]))
        far.append(passed_along(x, "ctx", 1))

    start = lax.axis_index("ctx") * ROWS
    front = SPAN * ROWS
    seg_pad = jnp.concatenate([jnp.full((front,), -1, jnp.int32), doc_ids[0]], axis=0)
    k_seg = lax.dynamic_slice_in_dim(seg_pad, start, front + ROWS)
    q_seg = k_seg[front:]
    feature = jnp.arange(128, dtype=jnp.int32)[None, :]
    f = ((feature <= q_seg[:, None]) & (feature < 64)).astype(jnp.bfloat16)
    t = jnp.where((feature > k_seg[:, None]) & (feature < 64), -FAR, 0.0).astype(jnp.bfloat16)
    sink_rows = jnp.repeat(sinks, TILE).reshape(H // 2, 2 * TILE)

    so_far, sums, sink_sums = None, [], []
    for c in range(CHUNKS):
        attended, grad_q, d2, d1, d0, sg = attend(
            c, queries, grads, (far[c], near[c], own[c]), f, t, sink_rows, so_far
        )
        so_far = (attended, grad_q)
        sums.append((d0, passed_along(d1, "ctx", -1), passed_along(d2, "ctx", -2)))
        sink_sums.append(jnp.sum(sg.reshape(-1, TILE), axis=1))
    sink_grad = jnp.concatenate(sink_sums)
    sink_grad, sums[:-1] = lax.optimization_barrier((sink_grad, sums[:-1]))
    grad_k, grad_v = [], []
    for d0, from_next, from_second in sums:
        total = d0 + from_next.astype(jnp.float32) + from_second.astype(jnp.float32)
        total = total.astype(jnp.bfloat16)
        for i in range(steps):
            grad_k.append(total[:, i * 256 : i * 256 + 128])
            grad_v.append(total[:, i * 256 + 128 : (i + 1) * 256])
    devices = lax.axis_size("dp") * lax.axis_size("ctx")
    spread = jnp.broadcast_to(sink_grad[None], (devices, H))
    sink_total = jnp.sum(lax.all_to_all(spread, ("dp", "ctx"), 0, 0, tiled=True), axis=0)
    return (
        attended[None],
        grad_q[None],
        jnp.concatenate(grad_k, axis=1)[None],
        jnp.concatenate(grad_v, axis=1)[None],
        sink_total,
    )


def solution(mesh):
    in_specs = (
        P("dp", "ctx", None),
        P("dp", "ctx", None),
        P("dp", "ctx", None),
        P(),
        P("dp", None),
        P("dp", "ctx", None),
    )
    out_specs = (
        P("dp", "ctx", None),
        P("dp", "ctx", None),
        P("dp", "ctx", None),
        P("dp", "ctx", None),
        P(),
    )
    return jax.shard_map(
        on_device, mesh=mesh, in_specs=in_specs, out_specs=out_specs, check_vma=False
    )
```

profile of v0, /device:TPU:1, one launch (start us, length us, event | category | flops | bytes accessed | tf_op | source)
XLA Modules:
  0.0 120.9 jit_solution(1013078776609845036)
XLA Ops:
  0.6 0.0 copy-start
  0.6 0.0 copy-start.1
  0.7 1.1 fusion.5
  1.8 4.4 %collective-permute-start.1 = (bf16[256,512]{1,0:T(8,128)(2,1)S(1)}, bf16[256,512]{1,0:T(8,128)(2,1)S(1)}, u32[]{:S(2)}, u32[]{:S(2)}) collective-permute-start(bf16[256,512]{1,0:T(8,128)(2,1)S(1)} %pad_maximum_fusion.1.refs_4_), channel_id=1, source_target_pairs={{0,1},{1,2},{2,3},{3,4},{4,5},{5,6},{6,7},{7,8},{8,9},{9,10},{10,1... | collective-permute-start | bytes 786440 | tf_op jit(solution)/shard_map/ppermute | solution.py:27
  6.3 3.5 %collective-permute-start = (bf16[256,512]{1,0:T(8,128)(2,1)S(1)}, bf16[256,512]{1,0:T(8,128)(2,1)S(1)}, u32[]{:S(2)}, u32[]{:S(2)}) collective-permute-start(bf16[256,512]{1,0:T(8,128)(2,1)S(1)} %pad_maximum_fusion.refs_4_), channel_id=1, source_target_pairs={{0,1},{1,2},{2,3},{3,4},{4,5},{5,6},{6,7},{7,8},{8,9},{9,10},{10,1... | collective-permute-start | bytes 786440 | tf_op jit(solution)/shard_map/ppermute | solution.py:27
  9.8 0.0 copy-done
  9.8 0.1 pad_dynamic-slice_fusion
  9.9 1.2 %collective-permute-done.1.refs_3_ = bf16[256,512]{1,0:T(8,128)(2,1)S(1)} collective-permute-done((bf16[256,512]{1,0:T(8,128)(2,1)S(1)}, bf16[256,512]{1,0:T(8,128)(2,1)S(1)}, u32[]{:S(2)}, u32[]{:S(2)}) %collective-permute-start.1) | collective-permute-done | bytes 262176 | tf_op jit(solution)/shard_map/ppermute | solution.py:27
  11.2 4.1 %collective-permute-start.2 = (bf16[256,512]{1,0:T(8,128)(2,1)S(1)}, bf16[256,512]{1,0:T(8,128)(2,1)S(1)}, u32[]{:S(2)}, u32[]{:S(2)}) collective-permute-start(bf16[256,512]{1,0:T(8,128)(2,1)S(1)} %collective-permute-done.1.refs_3_), channel_id=1, source_target_pairs={{0,1},{1,2},{2,3},{3,4},{4,5},{5,6},{6,7},{7,8},{8,9},{9,10},{10,1... | collective-permute-start | bytes 786440 | tf_op jit(solution)/shard_map/ppermute | solution.py:27
  15.3 0.1 fusion.2.refs_5_
  15.4 0.0 copy-done.1
  15.4 0.1 broadcast_in_dim.39
  15.5 0.1 broadcast_in_dim.40
  15.6 0.2 select_convert_fusion.refs_6_
  15.8 1.0 collective-permute-done.refs_3_
  16.8 5.6 %collective-permute-done.2.refs_2_ = bf16[256,512]{1,0:T(8,128)(2,1)S(1)} collective-permute-done((bf16[256,512]{1,0:T(8,128)(2,1)S(1)}, bf16[256,512]{1,0:T(8,128)(2,1)S(1)}, u32[]{:S(2)}, u32[]{:S(2)}) %collective-permute-start.2) | collective-permute-done | bytes 262176 | tf_op jit(solution)/shard_map/ppermute | solution.py:27
  22.4 4.1 %collective-permute-start.3 = (bf16[256,512]{1,0:T(8,128)(2,1)S(1)}, bf16[256,512]{1,0:T(8,128)(2,1)S(1)}, u32[]{:S(2)}, u32[]{:S(2)}) collective-permute-start(bf16[256,512]{1,0:T(8,128)(2,1)S(1)} %collective-permute-done.refs_3_), channel_id=1, source_target_pairs={{0,1},{1,2},{2,3},{3,4},{4,5},{5,6},{6,7},{7,8},{8,9},{9,10},{10,1... | collective-permute-start | bytes 786440 | tf_op jit(solution)/shard_map/ppermute | solution.py:27
  26.5 20.2 %shard_map.101 = (bf16[256,4096]{1,0:T(8,128)(2,1)}, bf16[256,4096]{1,0:T(8,128)(2,1)}, bf16[256,512]{1,0:T(8,128)(2,1)S(1)}, bf16[256,512]{1,0:T(8,128)(2,1)S(1...) custom-call(bf16[256,4096]{1,0:T(8,128)(2,1)} %bitcast.21, bf16[256,4096]{1,0:T(8,128)(2,1)} %bitcast.23, ...), custom_call_target="tpu_custom_call" | custom-call | flops 16106127360 | bytes 2097152 | tf_op jit(solution)/shard_map/pallas_call | solution.py:189
  46.7 1.3 %collective-permute-start.4 = (bf16[256,512]{1,0:T(8,128)(2,1)S(1)}, bf16[256,512]{1,0:T(8,128)(2,1)S(1)}, u32[]{:S(2)}, u32[]{:S(2)}) collective-permute-start(bf16[256,512]{1,0:T(8,128)(2,1)S(1)} %get-tuple-element.32), channel_id=1, source_target_pairs={{1,0},{2,1},{3,2},{4,3},{5,4},{6,5},{7,6},{8,7},{9,8},{10,9},{11,1... | collective-permute-start | bytes 786440 | tf_op jit(solution)/shard_map/ppermute | solution.py:27
  48.0 1.5 %collective-permute-start.5 = (bf16[256,512]{1,0:T(8,128)(2,1)S(1)}, bf16[256,512]{1,0:T(8,128)(2,1)}, u32[]{:S(2)}, u32[]{:S(2)}) collective-permute-start(bf16[256,512]{1,0:T(8,128)(2,1)S(1)} %get-tuple-element.33), channel_id=1, source_target_pairs={{2,0},{3,1},{4,2},{5,3},{6,4},{7,5},{8,6},{9,7},{10,8},{11,9},{12,... | collective-permute-start | bytes 786440 | tf_op jit(solution)/shard_map/ppermute | solution.py:27
  49.5 0.1 reduce_sum.27
  49.6 0.0 collective-permute-done.3.refs_2_
  49.6 20.2 %shard_map.102 = (bf16[256,4096]{1,0:T(8,128)(2,1)}, bf16[256,4096]{1,0:T(8,128)(2,1)}, bf16[256,512]{1,0:T(8,128)(2,1)S(1)}, bf16[256,512]{1,0:T(8,128)(2,1)S(1...) custom-call(bf16[256,4096]{1,0:T(8,128)(2,1)} %bitcast.22, ...), custom_call_target="tpu_custom_call", output_to_operand_aliasing={{0}: (8, {}), {1}: (9, {})} | custom-call | flops 16106127360 | bytes 2097152 | tf_op jit(solution)/shard_map/pallas_call | solution.py:189
  69.8 0.1 reduce_sum.28
  69.9 1.3 %collective-permute-start.6 = (bf16[256,512]{1,0:T(8,128)(2,1)S(1)}, bf16[256,512]{1,0:T(8,128)(2,1)S(1)}, u32[]{:S(2)}, u32[]{:S(2)}) collective-permute-start(bf16[256,512]{1,0:T(8,128)(2,1)S(1)} %get-tuple-element.38), channel_id=1, source_target_pairs={{1,0},{2,1},{3,2},{4,3},{5,4},{6,5},{7,6},{8,7},{9,8},{10,9},{11,1... | collective-permute-start | bytes 786440 | tf_op jit(solution)/shard_map/ppermute | solution.py:27
  71.2 1.3 %collective-permute-start.7 = (bf16[256,512]{1,0:T(8,128)(2,1)S(1)}, bf16[256,512]{1,0:T(8,128)(2,1)S(1)}, u32[]{:S(2)}, u32[]{:S(2)}) collective-permute-start(bf16[256,512]{1,0:T(8,128)(2,1)S(1)} %get-tuple-element.39), channel_id=1, source_target_pairs={{2,0},{3,1},{4,2},{5,3},{6,4},{7,5},{8,6},{9,7},{10,8},{11,9},{12,... | collective-permute-start | bytes 786440 | tf_op jit(solution)/shard_map/ppermute | solution.py:27
  72.5 0.1 pad_maximum_fusion.2
  72.6 0.0 collective-permute-done.4
  72.6 0.0 collective-permute-done.5
  72.6 0.7 broadcast_in_dim.46
  73.3 32.4 %all-to-all-start = ((f32[256,1,64]{2,1,0:T(1,128)}), f32[256,1,64]{2,1,0:T(1,128)S(1)}, u32[]{:S(2)}, u32[]{:S(2)}) async-start(f32[256,1,64]{2,1,0:T(1,128)} %broadcast_in_dim.46), calls=%async_computation | async-start | bytes 262144 | tf_op jit(solution)/shard_map/all_to_all | solution.py:270
  105.7 1.1 add_convert_fusion.1
  106.8 11.6 %all-to-all-done = f32[256,1,64]{2,1,0:T(1,128)S(1)} async-done(((f32[256,1,64]{2,1,0:T(1,128)}), f32[256,1,64]{2,1,0:T(1,128)S(1)}, u32[]{:S(2)}, u32[]{:S(2)}) %all-to-all-start) | async-done | bytes 65568 | tf_op jit(solution)/shard_map/all_to_all | solution.py:270
  118.5 0.8 reduce_sum.29
  119.3 0.0 collective-permute-done.6
  119.3 0.0 collective-permute-done.7
  119.3 0.1 add_convert_fusion
  119.4 0.7 maximum_bitcast_fusion.1
  120.2 0.7 maximum_bitcast_fusion
  (9 shorter events, 0.2 us)
Async XLA Ops:
  0.6 9.2 %copy-start = (s32[1,16384]{1,0:T(1,128)S(1)}, s32[1,16384]{1,0:T(1,128)}, u32[]{:S(2)}) copy-start(s32[1,16384]{1,0:T(1,128)} %param.10) | copy-start | bytes 196612
  0.6 14.8 %copy-start.1 = (f32[64]{0:T(128)S(1)}, f32[64]{0:T(128)}, u32[]{:S(2)}) copy-start(f32[64]{0:T(128)} %param.9) | copy-start | bytes 772
  1.8 9.3 %collective-permute-start.1 = (bf16[256,512]{1,0:T(8,128)(2,1)S(1)}, bf16[256,512]{1,0:T(8,128)(2,1)S(1)}, u32[]{:S(2)}, u32[]{:S(2)}) collective-permute-start(bf16[256,512]{1,0:T(8,128)(2,1)S(1)} %pad_maximum_fusion.1.refs_4_), channel_id=1, source_target_pairs={{0,1},{1,2},{2,3},{3,4},{4,5},{5,6},{6,7},{7,8},{8,9},{9,10},{10,1... | collective-permute-start | bytes 786440 | tf_op jit(solution)/shard_map/ppermute | solution.py:27
  6.3 10.5 %collective-permute-start = (bf16[256,512]{1,0:T(8,128)(2,1)S(1)}, bf16[256,512]{1,0:T(8,128)(2,1)S(1)}, u32[]{:S(2)}, u32[]{:S(2)}) collective-permute-start(bf16[256,512]{1,0:T(8,128)(2,1)S(1)} %pad_maximum_fusion.refs_4_), channel_id=1, source_target_pairs={{0,1},{1,2},{2,3},{3,4},{4,5},{5,6},{6,7},{7,8},{8,9},{9,10},{10,1... | collective-permute-start | bytes 786440 | tf_op jit(solution)/shard_map/ppermute | solution.py:27
  11.2 11.2 %collective-permute-start.2 = (bf16[256,512]{1,0:T(8,128)(2,1)S(1)}, bf16[256,512]{1,0:T(8,128)(2,1)S(1)}, u32[]{:S(2)}, u32[]{:S(2)}) collective-permute-start(bf16[256,512]{1,0:T(8,128)(2,1)S(1)} %collective-permute-done.1.refs_3_), channel_id=1, source_target_pairs={{0,1},{1,2},{2,3},{3,4},{4,5},{5,6},{6,7},{7,8},{8,9},{9,10},{10,1... | collective-permute-start | bytes 786440 | tf_op jit(solution)/shard_map/ppermute | solution.py:27
  22.4 27.2 %collective-permute-start.3 = (bf16[256,512]{1,0:T(8,128)(2,1)S(1)}, bf16[256,512]{1,0:T(8,128)(2,1)S(1)}, u32[]{:S(2)}, u32[]{:S(2)}) collective-permute-start(bf16[256,512]{1,0:T(8,128)(2,1)S(1)} %collective-permute-done.refs_3_), channel_id=1, source_target_pairs={{0,1},{1,2},{2,3},{3,4},{4,5},{5,6},{6,7},{7,8},{8,9},{9,10},{10,1... | collective-permute-start | bytes 786440 | tf_op jit(solution)/shard_map/ppermute | solution.py:27
  46.7 25.9 %collective-permute-start.4 = (bf16[256,512]{1,0:T(8,128)(2,1)S(1)}, bf16[256,512]{1,0:T(8,128)(2,1)S(1)}, u32[]{:S(2)}, u32[]{:S(2)}) collective-permute-start(bf16[256,512]{1,0:T(8,128)(2,1)S(1)} %get-tuple-element.32), channel_id=1, source_target_pairs={{1,0},{2,1},{3,2},{4,3},{5,4},{6,5},{7,6},{8,7},{9,8},{10,9},{11,1... | collective-permute-start | bytes 786440 | tf_op jit(solution)/shard_map/ppermute | solution.py:27
  48.0 24.6 %collective-permute-start.5 = (bf16[256,512]{1,0:T(8,128)(2,1)S(1)}, bf16[256,512]{1,0:T(8,128)(2,1)}, u32[]{:S(2)}, u32[]{:S(2)}) collective-permute-start(bf16[256,512]{1,0:T(8,128)(2,1)S(1)} %get-tuple-element.33), channel_id=1, source_target_pairs={{2,0},{3,1},{4,2},{5,3},{6,4},{7,5},{8,6},{9,7},{10,8},{11,9},{12,... | collective-permute-start | bytes 786440 | tf_op jit(solution)/shard_map/ppermute | solution.py:27
  69.9 49.3 %collective-permute-start.6 = (bf16[256,512]{1,0:T(8,128)(2,1)S(1)}, bf16[256,512]{1,0:T(8,128)(2,1)S(1)}, u32[]{:S(2)}, u32[]{:S(2)}) collective-permute-start(bf16[256,512]{1,0:T(8,128)(2,1)S(1)} %get-tuple-element.38), channel_id=1, source_target_pairs={{1,0},{2,1},{3,2},{4,3},{5,4},{6,5},{7,6},{8,7},{9,8},{10,9},{11,1... | collective-permute-start | bytes 786440 | tf_op jit(solution)/shard_map/ppermute | solution.py:27
  71.2 48.0 %collective-permute-start.7 = (bf16[256,512]{1,0:T(8,128)(2,1)S(1)}, bf16[256,512]{1,0:T(8,128)(2,1)S(1)}, u32[]{:S(2)}, u32[]{:S(2)}) collective-permute-start(bf16[256,512]{1,0:T(8,128)(2,1)S(1)} %get-tuple-element.39), channel_id=1, source_target_pairs={{2,0},{3,1},{4,2},{5,3},{6,4},{7,5},{8,6},{9,7},{10,8},{11,9},{12,... | collective-permute-start | bytes 786440 | tf_op jit(solution)/shard_map/ppermute | solution.py:27
  73.3 45.1 %all-to-all-start = ((f32[256,1,64]{2,1,0:T(1,128)}), f32[256,1,64]{2,1,0:T(1,128)S(1)}, u32[]{:S(2)}, u32[]{:S(2)}) async-start(f32[256,1,64]{2,1,0:T(1,128)} %broadcast_in_dim.46), calls=%async_computation | async-start | bytes 262144 | tf_op jit(solution)/shard_map/all_to_all | solution.py:270
where the time goes:
time: 121 us
  starting transfers between devices  53.9 us (45%)
  Pallas kernels  40.4 us (33%)
  waiting for transfers between devices  19.5 us (16%)
  other arithmetic  4.07 us (3%)
  local copies, waits for them, and re-layouts  2.26 us (2%)
    pallas_call x2, Pallas kernels, attend(): pl.pallas_call(functools.partial(kernel, so_far is None), grid=(steps,),...  40.4 us
    all_to_all x1, starting transfers between devices, on_device(): lax.all_to_all(spread, ('dp', 'ctx'), 0, 0, tiled=True)  32.4 us
    ppermute x8, starting transfers between devices, passed_along(): return lax.ppermute(block, axis, route)  21.5 us
    all_to_all x1, waiting for transfers between devices, on_device(): lax.all_to_all(spread, ('dp', 'ctx'), 0, 0, tiled=True)  11.6 us
    ppermute x8, waiting for transfers between devices, passed_along(): return lax.ppermute(block, axis, route)  7.86 us
  transfers between devices with their start and end apart: 9, of which 4 were waited for; matrix products, arithmetic and copies ran while one was open for 3% of the time, Pallas kernels for 33%

commit v1 on v0

--- a/solution.py
+++ b/solution.py
@@ -195,7 +195,7 @@
             pltpu.HBM((ROWS, H * HD), bf),
             pltpu.HBM((ROWS, H * HD), bf),
             jax.ShapeDtypeStruct((ROWS, 256 * steps), bf),
-            jax.ShapeDtypeStruct((ROWS, 256 * steps), bf),
+            jax.ShapeDtypeStruct((ROWS, 256 * steps), f32),
             jax.ShapeDtypeStruct((ROWS, 256 * steps), f32),
             jax.ShapeDtypeStruct((8 * steps, 256), f32),
         ],
@@ -248,26 +248,36 @@
     t = jnp.where((feature > k_seg[:, None]) & (feature < 64), -FAR, 0.0).astype(jnp.bfloat16)
     sink_rows = jnp.repeat(sinks, TILE).reshape(H // 2, 2 * TILE)
 
-    so_far, sums, sink_sums = None, [], []
+    so_far, parts = None, []
     for c in range(CHUNKS):
-        attended, grad_q, d2, d1, d0, sg = attend(
+        attended, grad_q, *rest = attend(
             c, queries, grads, (far[c], near[c], own[c]), f, t, sink_rows, so_far
         )
         so_far = (attended, grad_q)
-        sums.append((d0, passed_along(d1, "ctx", -1), passed_along(d2, "ctx", -2)))
-        sink_sums.append(jnp.sum(sg.reshape(-1, TILE), axis=1))
-    sink_grad = jnp.concatenate(sink_sums)
-    sink_grad, sums[:-1] = lax.optimization_barrier((sink_grad, sums[:-1]))
+        parts.append(rest)
+        if c == 0:
+            got = passed_along(rest[0], "ctx", -1)
+    (_, near_0, own_0, sinks_0), (far_1, near_1, own_1, sinks_1) = parts
+
+    def joined(share, came):
+        return (share + came.astype(jnp.float32)).astype(jnp.bfloat16)
+
+    half = 256 * steps
+    got, far_1 = lax.optimization_barrier((got, far_1))
+    both = jnp.concatenate([far_1, joined(near_0, got)], axis=1)
+    both = passed_along(both, "ctx", -1)
+    sink_grad = jnp.concatenate([jnp.sum(x.reshape(-1, TILE), axis=1) for x in (sinks_0, sinks_1)])
+    devices = lax.axis_size("dp") * lax.axis_size("ctx")
+    spread = jnp.broadcast_to(sink_grad[None], (devices, H))
+    spread = lax.all_to_all(spread, ("dp", "ctx"), 0, 0, tiled=True)
+    both, spread = lax.optimization_barrier((both, spread))
+    last = passed_along(joined(near_1, both[:, :half]), "ctx", -1)
+    sink_total = jnp.sum(spread, axis=0)
     grad_k, grad_v = [], []
-    for d0, from_next, from_second in sums:
-        total = d0 + from_next.astype(jnp.float32) + from_second.astype(jnp.float32)
-        total = total.astype(jnp.bfloat16)
+    for total in (joined(own_0, both[:, half:]), joined(own_1, last)):
         for i in range(steps):
             grad_k.append(total[:, i * 256 : i * 256 + 128])
             grad_v.append(total[:, i * 256 + 128 : (i + 1) * 256])
-    devices = lax.axis_size("dp") * lax.axis_size("ctx")
-    spread = jnp.broadcast_to(sink_grad[None], (devices, H))
-    sink_total = jnp.sum(lax.all_to_all(spread, ("dp", "ctx"), 0, 0, tiled=True), axis=0)
     return (
         attended[None],
         grad_q[None],

time: 121 us -> 120 us (level)
  blocking collectives: 0 us -> 38.7 us
  starting transfers between devices: 53.9 us -> 20.2 us
  waiting for transfers between devices: 19.5 us -> 14.9 us
    all_to_all x0 -> x1, blocking collectives: none -> 38.7 us  [on_device(): spread = lax.all_to_all(spread, ('dp', 'ctx'), 0, 0, tiled=True)]
    all_to_all x1 -> x0, starting transfers between devices: 32.4 us -> none  [on_device(): lax.all_to_all(spread, ('dp', 'ctx'), 0, 0, tiled=True)]
    all_to_all x1 -> x0, waiting for transfers between devices: 11.6 us -> none  [on_device(): lax.all_to_all(spread, ('dp', 'ctx'), 0, 0, tiled=True)]
    ppermute x8 -> x7, waiting for transfers between devices: 7.86 us -> 14.9 us  [passed_along(): return lax.ppermute(block, axis, route)]
    ppermute x8 -> x7, starting transfers between devices: 21.5 us -> 20.2 us  [passed_along(): return lax.ppermute(block, axis, route)]
  transfers between devices with their start and end apart: 9 -> 7, of which waited for: 4 -> 4; matrix products, arithmetic and copies ran while one was open for 3% -> 1% of each run, Pallas kernels for 33% -> 34%
where the time goes in v1:
time: 120 us
  Pallas kernels  40.4 us (34%)
  blocking collectives  38.7 us (32%)
  starting transfers between devices  20.2 us (17%)
  waiting for transfers between devices  14.9 us (12%)
  other arithmetic  3.04 us (3%)
  local copies, waits for them, and re-layouts  1.61 us (1%)
    pallas_call x2, Pallas kernels, attend(): pl.pallas_call(functools.partial(kernel, so_far is None), grid=(steps,),...  40.4 us
    all_to_all x1, blocking collectives, on_device(): spread = lax.all_to_all(spread, ('dp', 'ctx'), 0, 0, tiled=True)  38.7 us
    ppermute x7, starting transfers between devices, passed_along(): return lax.ppermute(block, axis, route)  20.2 us
    ppermute x7, waiting for transfers between devices, passed_along(): return lax.ppermute(block, axis, route)  14.9 us
  transfers between devices with their start and end apart: 7, of which 4 were waited for; matrix products, arithmetic and copies ran while one was open for 1% of the time, Pallas kernels for 34%

profile of v1, /device:TPU:1, one launch (start us, length us, event | category | flops | bytes accessed | tf_op | source)
XLA Modules:
  0.0 119.7 jit_solution(5468125991168953217)
XLA Ops:
  0.6 0.0 copy-start
  0.6 0.0 copy-start.1
  0.7 1.1 fusion.5
  1.8 4.4 %collective-permute-start.1 = (bf16[256,512]{1,0:T(8,128)(2,1)S(1)}, bf16[256,512]{1,0:T(8,128)(2,1)S(1)}, u32[]{:S(2)}, u32[]{:S(2)}) collective-permute-start(bf16[256,512]{1,0:T(8,128)(2,1)S(1)} %pad_maximum_fusion.2.refs_4_), channel_id=1, source_target_pairs={{0,1},{1,2},{2,3},{3,4},{4,5},{5,6},{6,7},{7,8},{8,9},{9,10},{10,1... | collective-permute-start | bytes 786440 | tf_op jit(solution)/shard_map/ppermute | solution.py:27
  6.3 3.5 %collective-permute-start = (bf16[256,512]{1,0:T(8,128)(2,1)S(1)}, bf16[256,512]{1,0:T(8,128)(2,1)S(1)}, u32[]{:S(2)}, u32[]{:S(2)}) collective-permute-start(bf16[256,512]{1,0:T(8,128)(2,1)S(1)} %pad_maximum_fusion.1.refs_4_), channel_id=1, source_target_pairs={{0,1},{1,2},{2,3},{3,4},{4,5},{5,6},{6,7},{7,8},{8,9},{9,10},{10,1... | collective-permute-start | bytes 786440 | tf_op jit(solution)/shard_map/ppermute | solution.py:27
  9.8 0.0 copy-done
  9.8 0.1 pad_dynamic-slice_fusion
  9.9 1.2 %collective-permute-done.1.refs_3_ = bf16[256,512]{1,0:T(8,128)(2,1)S(1)} collective-permute-done((bf16[256,512]{1,0:T(8,128)(2,1)S(1)}, bf16[256,512]{1,0:T(8,128)(2,1)S(1)}, u32[]{:S(2)}, u32[]{:S(2)}) %collective-permute-start.1) | collective-permute-done | bytes 262176 | tf_op jit(solution)/shard_map/ppermute | solution.py:27
  11.2 4.1 %collective-permute-start.2 = (bf16[256,512]{1,0:T(8,128)(2,1)S(1)}, bf16[256,512]{1,0:T(8,128)(2,1)S(1)}, u32[]{:S(2)}, u32[]{:S(2)}) collective-permute-start(bf16[256,512]{1,0:T(8,128)(2,1)S(1)} %collective-permute-done.1.refs_3_), channel_id=1, source_target_pairs={{0,1},{1,2},{2,3},{3,4},{4,5},{5,6},{6,7},{7,8},{8,9},{9,10},{10,1... | collective-permute-start | bytes 786440 | tf_op jit(solution)/shard_map/ppermute | solution.py:27
  15.3 0.1 fusion.2.refs_5_
  15.4 0.0 copy-done.1
  15.4 0.1 broadcast_in_dim.39
  15.5 0.1 broadcast_in_dim.40
  15.6 0.2 select_convert_fusion.refs_6_
  15.8 1.0 collective-permute-done.refs_3_
  16.8 5.6 %collective-permute-done.2.refs_2_ = bf16[256,512]{1,0:T(8,128)(2,1)S(1)} collective-permute-done((bf16[256,512]{1,0:T(8,128)(2,1)S(1)}, bf16[256,512]{1,0:T(8,128)(2,1)S(1)}, u32[]{:S(2)}, u32[]{:S(2)}) %collective-permute-start.2) | collective-permute-done | bytes 262176 | tf_op jit(solution)/shard_map/ppermute | solution.py:27
  22.4 4.1 %collective-permute-start.3 = (bf16[256,512]{1,0:T(8,128)(2,1)S(1)}, bf16[256,512]{1,0:T(8,128)(2,1)S(1)}, u32[]{:S(2)}, u32[]{:S(2)}) collective-permute-start(bf16[256,512]{1,0:T(8,128)(2,1)S(1)} %collective-permute-done.refs_3_), channel_id=1, source_target_pairs={{0,1},{1,2},{2,3},{3,4},{4,5},{5,6},{6,7},{7,8},{8,9},{9,10},{10,1... | collective-permute-start | bytes 786440 | tf_op jit(solution)/shard_map/ppermute | solution.py:27
  26.5 20.2 %shard_map.101 = (bf16[256,4096]{1,0:T(8,128)(2,1)}, bf16[256,4096]{1,0:T(8,128)(2,1)}, bf16[256,512]{1,0:T(8,128)(2,1)S(1)}, f32[256,512]{1,0:T(8,128)S(1)}, f3...) custom-call(bf16[256,4096]{1,0:T(8,128)(2,1)} %bitcast.23, bf16[256,4096]{1,0:T(8,128)(2,1)} %bitcast.25, ...), custom_call_target="tpu_custom_call" | custom-call | flops 16106127360 | bytes 2097152 | tf_op jit(solution)/shard_map/pallas_call | solution.py:189
  46.7 1.5 %collective-permute-start.4 = (bf16[256,512]{1,0:T(8,128)(2,1)S(1)}, bf16[256,512]{1,0:T(8,128)(2,1)S(1)}, u32[]{:S(2)}, u32[]{:S(2)}) collective-permute-start(bf16[256,512]{1,0:T(8,128)(2,1)S(1)} %get-tuple-element.30), channel_id=1, source_target_pairs={{1,0},{2,1},{3,2},{4,3},{5,4},{6,5},{7,6},{8,7},{9,8},{10,9},{11,1... | collective-permute-start | bytes 786440 | tf_op jit(solution)/shard_map/ppermute | solution.py:27
  48.2 0.0 collective-permute-done.3.refs_2_
  48.2 20.2 %shard_map.102 = (bf16[256,4096]{1,0:T(8,128)(2,1)}, bf16[256,4096]{1,0:T(8,128)(2,1)}, bf16[256,512]{1,0:T(8,128)(2,1)S(1)}, f32[256,512]{1,0:T(8,128)S(1)}, f3...) custom-call(bf16[256,4096]{1,0:T(8,128)(2,1)} %bitcast.24, ...), custom_call_target="tpu_custom_call", output_to_operand_aliasing={{0}: (8, {}), {1}: (9, {})} | custom-call | flops 16106127360 | bytes 2097152 | tf_op jit(solution)/shard_map/pallas_call | solution.py:189
  68.4 0.0 collective-permute-done.4
  68.4 0.1 add_convert_fusion.3
  68.5 0.1 pad_maximum_fusion
  68.6 1.3 %collective-permute-start.5 = (bf16[256,1024]{1,0:T(8,128)(2,1)S(1)}, bf16[256,1024]{1,0:T(8,128)(2,1)S(1)}, u32[]{:S(2)}, u32[]{:S(2)}) collective-permute-start(bf16[256,1024]{1,0:T(8,128)(2,1)S(1)} %pad_maximum_fusion), channel_id=1, source_target_pairs={{1,0},{2,1},{3,2},{4,3},{5,4},{6,5},{7,6},{8,7},{9,8},{10,9},{11,1... | collective-permute-start | bytes 1572872 | tf_op jit(solution)/shard_map/ppermute | solution.py:27
  69.9 0.1 reduce_sum.27
  70.0 0.1 reduce_sum.28
  70.1 0.1 pad_maximum_fusion.3
  70.2 0.1 broadcast_in_dim.44
  70.3 38.7 %all_to_all.9 = f32[256,1,64]{2,1,0:T(1,128)S(1)} all-to-all(f32[256,1,64]{2,1,0:T(1,128)S(1)} %broadcast_in_dim.44), channel_id=1, replica_groups=mesh['dp'=4,'ctx'=64] {'dp','ctx'}, dimensions={0} | all-to-all | bytes 131072 | tf_op jit(solution)/shard_map/all_to_all | solution.py:272
  109.0 0.0 collective-permute-done.5
  109.0 0.2 add_convert_fusion.2
  109.2 1.3 %collective-permute-start.6 = (bf16[256,512]{1,0:T(8,128)(2,1)S(1)}, bf16[256,512]{1,0:T(8,128)(2,1)S(1)}, u32[]{:S(2)}, u32[]{:S(2)}) collective-permute-start(bf16[256,512]{1,0:T(8,128)(2,1)S(1)} %get-tuple-element.42), channel_id=1, source_target_pairs={{1,0},{2,1},{3,2},{4,3},{5,4},{6,5},{7,6},{8,7},{9,8},{10,9},{11,1... | collective-permute-start | bytes 786440 | tf_op jit(solution)/shard_map/ppermute | solution.py:27
  110.5 0.6 reduce_sum.29
  111.1 7.0 %collective-permute-done.6 = bf16[256,512]{1,0:T(8,128)(2,1)S(1)} collective-permute-done((bf16[256,512]{1,0:T(8,128)(2,1)S(1)}, bf16[256,512]{1,0:T(8,128)(2,1)S(1)}, u32[]{:S(2)}, u32[]{:S(2)}) %collective-permute-start.6) | collective-permute-done | bytes 262176 | tf_op jit(solution)/shard_map/ppermute | solution.py:27
  118.1 0.1 add_convert_fusion
  118.2 0.7 maximum_bitcast_fusion.1
  119.0 0.7 maximum_bitcast_fusion
  (9 shorter events, 0.2 us)
Async XLA Ops:
  0.6 9.2 %copy-start = (s32[1,16384]{1,0:T(1,128)S(1)}, s32[1,16384]{1,0:T(1,128)}, u32[]{:S(2)}) copy-start(s32[1,16384]{1,0:T(1,128)} %param.10) | copy-start | bytes 196612
  0.6 14.8 %copy-start.1 = (f32[64]{0:T(128)S(1)}, f32[64]{0:T(128)}, u32[]{:S(2)}) copy-start(f32[64]{0:T(128)} %param.9) | copy-start | bytes 772
  1.8 9.3 %collective-permute-start.1 = (bf16[256,512]{1,0:T(8,128)(2,1)S(1)}, bf16[256,512]{1,0:T(8,128)(2,1)S(1)}, u32[]{:S(2)}, u32[]{:S(2)}) collective-permute-start(bf16[256,512]{1,0:T(8,128)(2,1)S(1)} %pad_maximum_fusion.2.refs_4_), channel_id=1, source_target_pairs={{0,1},{1,2},{2,3},{3,4},{4,5},{5,6},{6,7},{7,8},{8,9},{9,10},{10,1... | collective-permute-start | bytes 786440 | tf_op jit(solution)/shard_map/ppermute | solution.py:27
  6.3 10.5 %collective-permute-start = (bf16[256,512]{1,0:T(8,128)(2,1)S(1)}, bf16[256,512]{1,0:T(8,128)(2,1)S(1)}, u32[]{:S(2)}, u32[]{:S(2)}) collective-permute-start(bf16[256,512]{1,0:T(8,128)(2,1)S(1)} %pad_maximum_fusion.1.refs_4_), channel_id=1, source_target_pairs={{0,1},{1,2},{2,3},{3,4},{4,5},{5,6},{6,7},{7,8},{8,9},{9,10},{10,1... | collective-permute-start | bytes 786440 | tf_op jit(solution)/shard_map/ppermute | solution.py:27
  11.2 11.2 %collective-permute-start.2 = (bf16[256,512]{1,0:T(8,128)(2,1)S(1)}, bf16[256,512]{1,0:T(8,128)(2,1)S(1)}, u32[]{:S(2)}, u32[]{:S(2)}) collective-permute-start(bf16[256,512]{1,0:T(8,128)(2,1)S(1)} %collective-permute-done.1.refs_3_), channel_id=1, source_target_pairs={{0,1},{1,2},{2,3},{3,4},{4,5},{5,6},{6,7},{7,8},{8,9},{9,10},{10,1... | collective-permute-start | bytes 786440 | tf_op jit(solution)/shard_map/ppermute | solution.py:27
  22.4 25.8 %collective-permute-start.3 = (bf16[256,512]{1,0:T(8,128)(2,1)S(1)}, bf16[256,512]{1,0:T(8,128)(2,1)S(1)}, u32[]{:S(2)}, u32[]{:S(2)}) collective-permute-start(bf16[256,512]{1,0:T(8,128)(2,1)S(1)} %collective-permute-done.refs_3_), channel_id=1, source_target_pairs={{0,1},{1,2},{2,3},{3,4},{4,5},{5,6},{6,7},{7,8},{8,9},{9,10},{10,1... | collective-permute-start | bytes 786440 | tf_op jit(solution)/shard_map/ppermute | solution.py:27
  46.7 21.7 %collective-permute-start.4 = (bf16[256,512]{1,0:T(8,128)(2,1)S(1)}, bf16[256,512]{1,0:T(8,128)(2,1)S(1)}, u32[]{:S(2)}, u32[]{:S(2)}) collective-permute-start(bf16[256,512]{1,0:T(8,128)(2,1)S(1)} %get-tuple-element.30), channel_id=1, source_target_pairs={{1,0},{2,1},{3,2},{4,3},{5,4},{6,5},{7,6},{8,7},{9,8},{10,9},{11,1... | collective-permute-start | bytes 786440 | tf_op jit(solution)/shard_map/ppermute | solution.py:27
  68.6 40.4 %collective-permute-start.5 = (bf16[256,1024]{1,0:T(8,128)(2,1)S(1)}, bf16[256,1024]{1,0:T(8,128)(2,1)S(1)}, u32[]{:S(2)}, u32[]{:S(2)}) collective-permute-start(bf16[256,1024]{1,0:T(8,128)(2,1)S(1)} %pad_maximum_fusion), channel_id=1, source_target_pairs={{1,0},{2,1},{3,2},{4,3},{5,4},{6,5},{7,6},{8,7},{9,8},{10,9},{11,1... | collective-permute-start | bytes 1572872 | tf_op jit(solution)/shard_map/ppermute | solution.py:27
  109.2 8.9 %collective-permute-start.6 = (bf16[256,512]{1,0:T(8,128)(2,1)S(1)}, bf16[256,512]{1,0:T(8,128)(2,1)S(1)}, u32[]{:S(2)}, u32[]{:S(2)}) collective-permute-start(bf16[256,512]{1,0:T(8,128)(2,1)S(1)} %get-tuple-element.42), channel_id=1, source_target_pairs={{1,0},{2,1},{3,2},{4,3},{5,4},{6,5},{7,6},{8,7},{9,8},{10,9},{11,1... | collective-permute-start | bytes 786440 | tf_op jit(solution)/shard_map/ppermute | solution.py:27

commit v2 on v1

--- a/solution.py
+++ b/solution.py
@@ -233,10 +233,7 @@
         own.append(jnp.concatenate(parts, axis=1))
     near = [passed_along(x, "ctx", 1) for x in own]
     far = []
-    for c, x in enumerate(near):
-        if c > 0:
-            x, far[c - 1] = lax.optimization_barrier((x, far[c - 1]))
-        far.append(passed_along(x, "ctx", 1))
+    far = [passed_along(x, "ctx", 1) for x in near]
 
     start = lax.axis_index("ctx") * ROWS
     front = SPAN * ROWS

time: 120 us -> 112 us (0.933)
  blocking collectives: 38.7 us -> 34.6 us
  waiting for transfers between devices: 14.9 us -> 10.8 us
    ppermute x7, waiting for transfers between devices: 14.9 us -> 10.8 us  [passed_along(): return lax.ppermute(block, axis, route)]
    all_to_all x1, blocking collectives: 38.7 us -> 34.6 us  [on_device(): spread = lax.all_to_all(spread, ('dp', 'ctx'), 0, 0, tiled=True)]
  transfers between devices with their start and end apart: 7 -> 7, of which waited for: 4 -> 4; matrix products, arithmetic and copies ran while one was open for 1% -> 1% of each run, Pallas kernels for 34% -> 36%
where the time goes in v2:
time: 112 us; the launch traced here: 111 us
  Pallas kernels  40.4 us (36%)
  blocking collectives  34.6 us (31%)
  starting transfers between devices  20.2 us (18%)
  waiting for transfers between devices  10.8 us (10%)
  other arithmetic  3.04 us (3%)
  local copies, waits for them, and re-layouts  1.61 us (1%)
    pallas_call x2, Pallas kernels, attend(): pl.pallas_call(functools.partial(kernel, so_far is None), grid=(steps,),...  40.4 us
    all_to_all x1, blocking collectives, on_device(): spread = lax.all_to_all(spread, ('dp', 'ctx'), 0, 0, tiled=True)  34.6 us
    ppermute x7, starting transfers between devices, passed_along(): return lax.ppermute(block, axis, route)  20.2 us
    ppermute x7, waiting for transfers between devices, passed_along(): return lax.ppermute(block, axis, route)  10.8 us
  transfers between devices with their start and end apart: 7, of which 4 were waited for; matrix products, arithmetic and copies ran while one was open for 1% of the time, Pallas kernels for 36%

profile of v2, /device:TPU:1, one launch (start us, length us, event | category | flops | bytes accessed | tf_op | source)
XLA Modules:
  0.0 111.5 jit_solution(6085806918821779221)
XLA Ops:
  0.6 0.0 copy-start
  0.6 0.0 copy-start.1
  0.7 1.1 %fusion.5 = (bf16[256,128]{1,0:T(8,128)(2,1)S(1)}, bf16[256,128]{1,0:T(8,128)(2,1)S(1)}, bf16[256,128]{1,0:T(8,128)(2,1)S(1)}, bf16[256,128]{1,0:T(8,128)(2,1)S(...) fusion(bf16[256,512]{1,0:T(8,128)(2,1)} %bitcast.19, ...), kind=kLoop, calls=%fused_computation.21 | loop fusion | bytes 1048576 | tf_op jit(solution)/shard_map/slice | solution.py:232
  1.8 4.4 %collective-permute-start.2 = (bf16[256,512]{1,0:T(8,128)(2,1)S(1)}, bf16[256,512]{1,0:T(8,128)(2,1)S(1)}, u32[]{:S(2)}, u32[]{:S(2)}) collective-permute-start(bf16[256,512]{1,0:T(8,128)(2,1)S(1)} %pad_maximum_fusion.2.refs_4_), channel_id=1, source_target_pairs={{0,1},{1,2},{2,3},{3,4},{4,5},{5,6},{6,7},{7,8},{8,9},{9,10},{10,1... | collective-permute-start | bytes 786440 | tf_op jit(solution)/shard_map/ppermute | solution.py:27
  6.3 3.5 %collective-permute-start = (bf16[256,512]{1,0:T(8,128)(2,1)S(1)}, bf16[256,512]{1,0:T(8,128)(2,1)S(1)}, u32[]{:S(2)}, u32[]{:S(2)}) collective-permute-start(bf16[256,512]{1,0:T(8,128)(2,1)S(1)} %pad_maximum_fusion.1.refs_4_), channel_id=1, source_target_pairs={{0,1},{1,2},{2,3},{3,4},{4,5},{5,6},{6,7},{7,8},{8,9},{9,10},{10,1... | collective-permute-start | bytes 786440 | tf_op jit(solution)/shard_map/ppermute | solution.py:27
  9.8 0.0 copy-done
  9.8 0.1 pad_dynamic-slice_fusion
  9.9 1.2 %collective-permute-done.2.refs_3_ = bf16[256,512]{1,0:T(8,128)(2,1)S(1)} collective-permute-done((bf16[256,512]{1,0:T(8,128)(2,1)S(1)}, bf16[256,512]{1,0:T(8,128)(2,1)S(1)}, u32[]{:S(2)}, u32[]{:S(2)}) %collective-permute-start.2) | collective-permute-done | bytes 262176 | tf_op jit(solution)/shard_map/ppermute | solution.py:27
  11.2 4.1 %collective-permute-start.3 = (bf16[256,512]{1,0:T(8,128)(2,1)S(1)}, bf16[256,512]{1,0:T(8,128)(2,1)S(1)}, u32[]{:S(2)}, u32[]{:S(2)}) collective-permute-start(bf16[256,512]{1,0:T(8,128)(2,1)S(1)} %collective-permute-done.2.refs_3_), channel_id=1, source_target_pairs={{0,1},{1,2},{2,3},{3,4},{4,5},{5,6},{6,7},{7,8},{8,9},{9,10},{10,1... | collective-permute-start | bytes 786440 | tf_op jit(solution)/shard_map/ppermute | solution.py:27
  15.3 0.1 fusion.2.refs_5_
  15.4 0.0 copy-done.1
  15.4 0.1 broadcast_in_dim.39
  15.5 0.1 broadcast_in_dim.40
  15.6 0.2 select_convert_fusion.refs_6_
  15.8 1.0 collective-permute-done.refs_3_
  16.8 4.1 %collective-permute-start.1 = (bf16[256,512]{1,0:T(8,128)(2,1)S(1)}, bf16[256,512]{1,0:T(8,128)(2,1)S(1)}, u32[]{:S(2)}, u32[]{:S(2)}) collective-permute-start(bf16[256,512]{1,0:T(8,128)(2,1)S(1)} %collective-permute-done.refs_3_), channel_id=1, source_target_pairs={{0,1},{1,2},{2,3},{3,4},{4,5},{5,6},{6,7},{7,8},{8,9},{9,10},{10,1... | collective-permute-start | bytes 786440 | tf_op jit(solution)/shard_map/ppermute | solution.py:27
  20.9 1.5 %collective-permute-done.3.refs_2_ = bf16[256,512]{1,0:T(8,128)(2,1)S(1)} collective-permute-done((bf16[256,512]{1,0:T(8,128)(2,1)S(1)}, bf16[256,512]{1,0:T(8,128)(2,1)S(1)}, u32[]{:S(2)}, u32[]{:S(2)}) %collective-permute-start.3) | collective-permute-done | bytes 262176 | tf_op jit(solution)/shard_map/ppermute | solution.py:27
  22.4 20.2 %shard_map.101 = (bf16[256,4096]{1,0:T(8,128)(2,1)}, bf16[256,4096]{1,0:T(8,128)(2,1)}, bf16[256,512]{1,0:T(8,128)(2,1)S(1)}, f32[256,512]{1,0:T(8,128)S(1)}, f3...) custom-call(bf16[256,4096]{1,0:T(8,128)(2,1)} %bitcast.23, bf16[256,4096]{1,0:T(8,128)(2,1)} %bitcast.25, ...), custom_call_target="tpu_custom_call" | custom-call | flops 16106127360 | bytes 2097152 | tf_op jit(solution)/shard_map/pallas_call | solution.py:189
  42.6 1.5 %collective-permute-start.4 = (bf16[256,512]{1,0:T(8,128)(2,1)S(1)}, bf16[256,512]{1,0:T(8,128)(2,1)S(1)}, u32[]{:S(2)}, u32[]{:S(2)}) collective-permute-start(bf16[256,512]{1,0:T(8,128)(2,1)S(1)} %get-tuple-element.26), channel_id=1, source_target_pairs={{1,0},{2,1},{3,2},{4,3},{5,4},{6,5},{7,6},{8,7},{9,8},{10,9},{11,1... | collective-permute-start | bytes 786440 | tf_op jit(solution)/shard_map/ppermute | solution.py:27
  44.1 0.0 collective-permute-done.1.refs_2_
  44.1 20.2 %shard_map.102 = (bf16[256,4096]{1,0:T(8,128)(2,1)}, bf16[256,4096]{1,0:T(8,128)(2,1)}, bf16[256,512]{1,0:T(8,128)(2,1)S(1)}, f32[256,512]{1,0:T(8,128)S(1)}, f3...) custom-call(bf16[256,4096]{1,0:T(8,128)(2,1)} %bitcast.24, ...), custom_call_target="tpu_custom_call", output_to_operand_aliasing={{0}: (8, {}), {1}: (9, {})} | custom-call | flops 16106127360 | bytes 2097152 | tf_op jit(solution)/shard_map/pallas_call | solution.py:189
  64.3 0.0 collective-permute-done.4
  64.3 0.1 add_convert_fusion.3
  64.4 0.1 pad_maximum_fusion
  64.4 1.3 %collective-permute-start.5 = (bf16[256,1024]{1,0:T(8,128)(2,1)S(1)}, bf16[256,1024]{1,0:T(8,128)(2,1)S(1)}, u32[]{:S(2)}, u32[]{:S(2)}) collective-permute-start(bf16[256,1024]{1,0:T(8,128)(2,1)S(1)} %pad_maximum_fusion), channel_id=1, source_target_pairs={{1,0},{2,1},{3,2},{4,3},{5,4},{6,5},{7,6},{8,7},{9,8},{10,9},{11,1... | collective-permute-start | bytes 1572872 | tf_op jit(solution)/shard_map/ppermute | solution.py:27
  65.8 0.1 reduce_sum.27
  65.9 0.1 reduce_sum.28
  66.0 0.1 pad_maximum_fusion.3
  66.1 0.1 broadcast_in_dim.44
  66.1 34.6 %all_to_all.9 = f32[256,1,64]{2,1,0:T(1,128)S(1)} all-to-all(f32[256,1,64]{2,1,0:T(1,128)S(1)} %broadcast_in_dim.44), channel_id=1, replica_groups=mesh['dp'=4,'ctx'=64] {'dp','ctx'}, dimensions={0} | all-to-all | bytes 131072 | tf_op jit(solution)/shard_map/all_to_all | solution.py:269
  100.8 0.0 collective-permute-done.5
  100.8 0.2 add_convert_fusion.2
  101.0 1.3 %collective-permute-start.6 = (bf16[256,512]{1,0:T(8,128)(2,1)S(1)}, bf16[256,512]{1,0:T(8,128)(2,1)S(1)}, u32[]{:S(2)}, u32[]{:S(2)}) collective-permute-start(bf16[256,512]{1,0:T(8,128)(2,1)S(1)} %get-tuple-element.38), channel_id=1, source_target_pairs={{1,0},{2,1},{3,2},{4,3},{5,4},{6,5},{7,6},{8,7},{9,8},{10,9},{11,1... | collective-permute-start | bytes 786440 | tf_op jit(solution)/shard_map/ppermute | solution.py:27
  102.3 0.6 reduce_sum.29
  102.9 7.0 %collective-permute-done.6 = bf16[256,512]{1,0:T(8,128)(2,1)S(1)} collective-permute-done((bf16[256,512]{1,0:T(8,128)(2,1)S(1)}, bf16[256,512]{1,0:T(8,128)(2,1)S(1)}, u32[]{:S(2)}, u32[]{:S(2)}) %collective-permute-start.6) | collective-permute-done | bytes 262176 | tf_op jit(solution)/shard_map/ppermute | solution.py:27
  109.9 0.1 add_convert_fusion
  110.0 0.7 maximum_bitcast_fusion.1
  110.8 0.7 maximum_bitcast_fusion
  (9 shorter events, 0.2 us)
Async XLA Ops:
  0.6 9.2 %copy-start = (s32[1,16384]{1,0:T(1,128)S(1)}, s32[1,16384]{1,0:T(1,128)}, u32[]{:S(2)}) copy-start(s32[1,16384]{1,0:T(1,128)} %param.10) | copy-start | bytes 196612
  0.6 14.8 %copy-start.1 = (f32[64]{0:T(128)S(1)}, f32[64]{0:T(128)}, u32[]{:S(2)}) copy-start(f32[64]{0:T(128)} %param.9) | copy-start | bytes 772
  1.8 9.3 %collective-permute-start.2 = (bf16[256,512]{1,0:T(8,128)(2,1)S(1)}, bf16[256,512]{1,0:T(8,128)(2,1)S(1)}, u32[]{:S(2)}, u32[]{:S(2)}) collective-permute-start(bf16[256,512]{1,0:T(8,128)(2,1)S(1)} %pad_maximum_fusion.2.refs_4_), channel_id=1, source_target_pairs={{0,1},{1,2},{2,3},{3,4},{4,5},{5,6},{6,7},{7,8},{8,9},{9,10},{10,1... | collective-permute-start | bytes 786440 | tf_op jit(solution)/shard_map/ppermute | solution.py:27
  6.3 10.5 %collective-permute-start = (bf16[256,512]{1,0:T(8,128)(2,1)S(1)}, bf16[256,512]{1,0:T(8,128)(2,1)S(1)}, u32[]{:S(2)}, u32[]{:S(2)}) collective-permute-start(bf16[256,512]{1,0:T(8,128)(2,1)S(1)} %pad_maximum_fusion.1.refs_4_), channel_id=1, source_target_pairs={{0,1},{1,2},{2,3},{3,4},{4,5},{5,6},{6,7},{7,8},{8,9},{9,10},{10,1... | collective-permute-start | bytes 786440 | tf_op jit(solution)/shard_map/ppermute | solution.py:27
  11.2 11.2 %collective-permute-start.3 = (bf16[256,512]{1,0:T(8,128)(2,1)S(1)}, bf16[256,512]{1,0:T(8,128)(2,1)S(1)}, u32[]{:S(2)}, u32[]{:S(2)}) collective-permute-start(bf16[256,512]{1,0:T(8,128)(2,1)S(1)} %collective-permute-done.2.refs_3_), channel_id=1, source_target_pairs={{0,1},{1,2},{2,3},{3,4},{4,5},{5,6},{6,7},{7,8},{8,9},{9,10},{10,1... | collective-permute-start | bytes 786440 | tf_op jit(solution)/shard_map/ppermute | solution.py:27
  16.8 27.3 %collective-permute-start.1 = (bf16[256,512]{1,0:T(8,128)(2,1)S(1)}, bf16[256,512]{1,0:T(8,128)(2,1)S(1)}, u32[]{:S(2)}, u32[]{:S(2)}) collective-permute-start(bf16[256,512]{1,0:T(8,128)(2,1)S(1)} %collective-permute-done.refs_3_), channel_id=1, source_target_pairs={{0,1},{1,2},{2,3},{3,4},{4,5},{5,6},{6,7},{7,8},{8,9},{9,10},{10,1... | collective-permute-start | bytes 786440 | tf_op jit(solution)/shard_map/ppermute | solution.py:27
  42.6 21.7 %collective-permute-start.4 = (bf16[256,512]{1,0:T(8,128)(2,1)S(1)}, bf16[256,512]{1,0:T(8,128)(2,1)S(1)}, u32[]{:S(2)}, u32[]{:S(2)}) collective-permute-start(bf16[256,512]{1,0:T(8,128)(2,1)S(1)} %get-tuple-element.26), channel_id=1, source_target_pairs={{1,0},{2,1},{3,2},{4,3},{5,4},{6,5},{7,6},{8,7},{9,8},{10,9},{11,1... | collective-permute-start | bytes 786440 | tf_op jit(solution)/shard_map/ppermute | solution.py:27
  64.4 36.4 %collective-permute-start.5 = (bf16[256,1024]{1,0:T(8,128)(2,1)S(1)}, bf16[256,1024]{1,0:T(8,128)(2,1)S(1)}, u32[]{:S(2)}, u32[]{:S(2)}) collective-permute-start(bf16[256,1024]{1,0:T(8,128)(2,1)S(1)} %pad_maximum_fusion), channel_id=1, source_target_pairs={{1,0},{2,1},{3,2},{4,3},{5,4},{6,5},{7,6},{8,7},{9,8},{10,9},{11,1... | collective-permute-start | bytes 1572872 | tf_op jit(solution)/shard_map/ppermute | solution.py:27
  101.0 8.9 %collective-permute-start.6 = (bf16[256,512]{1,0:T(8,128)(2,1)S(1)}, bf16[256,512]{1,0:T(8,128)(2,1)S(1)}, u32[]{:S(2)}, u32[]{:S(2)}) collective-permute-start(bf16[256,512]{1,0:T(8,128)(2,1)S(1)} %get-tuple-element.38), channel_id=1, source_target_pairs={{1,0},{2,1},{3,2},{4,3},{5,4},{6,5},{7,6},{8,7},{9,8},{10,9},{11,1... | collective-permute-start | bytes 786440 | tf_op jit(solution)/shard_map/ppermute | solution.py:27
